TPU v7x, 32 devices: a whole 2x2x4 slice. The times are simulated.
32 devices in a mesh: ctx: 8 (over z, x), head: 4 (over y, core).
Axes of the slice: x: 2, y: 2, z: 4, core: 2. Of those that a mesh axis runs over, the one named last changes fastest.
Arguments:
- query: bfloat16 [1024, 2048], P('ctx', 'head'), may hold values from -5 to 5, as said below
- key: bfloat16 [1024, 128], P('ctx'), may hold values from -5 to 5, as said below
- value: bfloat16 [1024, 128], P('ctx'), may hold values from -6 to 6
- grad_out: bfloat16 [1024, 2048], P('ctx', 'head'), may hold values from -6 to 6
- doc_lengths: int32 [32], replicated, may hold values from 1 to 64, 1024 in all
Outputs:
- attention_out: bfloat16 [1024, 2048], P('ctx', 'head')
- grad_query: bfloat16 [1024, 2048], P('ctx', 'head')
- grad_key: bfloat16 [1024, 128], P('ctx')
- grad_value: bfloat16 [1024, 128], P('ctx')
Inputs may be any that keep to these rules, and one draw needn't show every extreme that they name: `doc_lengths`: positive lengths of the documents in sequence order, summing to 1024; the longest is exactly 64. `query`: real values. `key`: real values.
All inputs are finite; a program needn't handle non-finite values.
Results may differ from a plain program's by a relative error of at most 0.014.
Values may be sent and summed in bfloat16 or wider, within the bound.
A program may use at most 64 MiB of HBM per device.

v0:
```python
import jax
import jax.numpy as jnp
import numpy as np
from jax import lax
from jax.sharding import PartitionSpec as P


def from_behind(array, axis, by):
    size = lax.axis_size(axis)
    pairs = [(i, i + by) for i in range(size) if 0 <= i + by < size]
    return lax.ppermute(array, axis, pairs)


def fold_home(key_parts, upward):
    slot_count = key_parts.shape[0]
    slot_grads = jnp.concatenate(
        [jnp.zeros((1,) + key_parts.shape[1:], jnp.float32), key_parts], axis=0
    )
    for bit_index in range(slot_count.bit_length()):
        offset = 1 << bit_index
        moving_slots = np.array(
            [slot for slot in range(slot_count + 1) if slot & offset], dtype=np.int32
        )
        moving = slot_grads[moving_slots]
        if upward:
            arrived = from_behind(moving.astype(jnp.bfloat16), "ctx", offset).astype(moving.dtype)
        else:
            arrived = from_behind(moving.astype(jnp.bfloat16), "ctx", -offset).astype(moving.dtype)
        slot_grads = slot_grads.at[moving_slots].set(0.0)
        slot_grads = slot_grads.at[moving_slots - offset].add(arrived)
    return slot_grads[0]


def body(query, key, value, grad_out, doc_lengths):
    tok_dev = key.shape[0]
    stretch_len = tok_dev // 2
    head_width = key.shape[1]
    head_count = query.shape[1] // head_width
    score_scale = head_width ** (-0.5)
    n_context = lax.axis_size("ctx")
    reach_count = n_context // 8
    my_index = lax.axis_index("ctx")
    doc_ends = jnp.cumsum(doc_lengths)

    def positions(first_row, row_count):
        global_row = first_row + jnp.arange(row_count, dtype=jnp.int32)
        owner_index = global_row // tok_dev
        inner_row = global_row % tok_dev
        stretch_id = jnp.where(
            inner_row < stretch_len, owner_index, 2 * n_context - 1 - owner_index
        )
        seq_place = stretch_id * stretch_len + inner_row % stretch_len
        inside = (owner_index >= 0) & (owner_index < n_context)
        seq_place = jnp.where(inside, seq_place, -1)
        doc_ids = jnp.sum((doc_ends[None, :] <= seq_place[:, None]).astype(jnp.int32), axis=1)
        return (seq_place, doc_ids)

    q_place, q_docs = positions(my_index * tok_dev, tok_dev)
    packed = jnp.concatenate([key, value], axis=1)
    queries = query.reshape(tok_dev, head_count, head_width)
    cotangent = grad_out.reshape(tok_dev, head_count, head_width)
    q_spans = [(0, tok_dev)]

    def live_pairs(k_place, k_docs, q_start, q_count):
        return (
            (k_docs[None, :] == q_docs[q_start : q_start + q_count, None])
            & (k_place[None, :] <= q_place[q_start : q_start + q_count, None])
            & (k_place[None, :] >= 0)
        )

    def tile_scores(key_block):
        return (
            jnp.einsum("rhd,kd->hrk", queries, key_block, preferred_element_type=jnp.float32)
            * score_scale
        )

    def add_stats(running, kv_block, k_place, k_docs):
        row_max, row_sum = running
        key_block = kv_block[:, :head_width]
        q_start, q_count = q_spans[0]
        live_mask = live_pairs(k_place, k_docs, q_start, q_count)

        def tile_stats(q_start=q_start, q_count=q_count, live_mask=live_mask):
            scores = tile_scores(key_block)
            tile_peak = jnp.max(jnp.where(live_mask[None], scores, -1e30), axis=2)
            tile_mass = jnp.sum(
                jnp.where(live_mask[None], jnp.exp(scores - tile_peak[:, :, None]), 0.0), axis=2
            )
            return (tile_peak, tile_mass)

        tile_peak, tile_mass = tile_stats()
        old_max = row_max
        new_max = jnp.maximum(old_max, tile_peak)
        merged = row_sum * jnp.exp(old_max - new_max) + tile_mass * jnp.exp(tile_peak - new_max)
        row_sum = row_sum.at[:, q_start : q_start + q_count].set(merged)
        row_max = row_max.at[:, q_start : q_start + q_count].set(new_max)
        return (row_max, row_sum)

    def sweep(update, initial):
        running = update(initial, packed, q_place, q_docs)

        def cycle_step(carried, step_index):
            running, kv_lower, kv_upper = carried
            kv_lower = from_behind(kv_lower, "ctx", 1)
            kv_upper = from_behind(kv_upper, "ctx", -1)
            k_place, k_docs = positions((my_index - step_index) * tok_dev, tok_dev)
            running = update(running, kv_lower, k_place, k_docs)
            k_place, k_docs = positions((my_index + step_index) * tok_dev, tok_dev)
            running = update(running, kv_upper, k_place, k_docs)
            return ((running, kv_lower, kv_upper), None)

        (running, kv_lower, kv_upper), unused = lax.scan(
            cycle_step, (running, packed, packed), jnp.arange(1, reach_count + 1, dtype=jnp.int32)
        )
        return running

    initial_stats = (
        jnp.full((head_count, tok_dev), -1e30, jnp.float32),
        jnp.zeros((head_count, tok_dev), jnp.float32),
    )
    row_max, row_sum = sweep(add_stats, initial_stats)
    log_sum = row_max + jnp.log(row_sum)

    def add_output(out_acc, kv_block, k_place, k_docs):
        key_block = kv_block[:, :head_width]
        value_block = kv_block[:, head_width:]
        q_start, q_count = q_spans[0]
        live_mask = live_pairs(k_place, k_docs, q_start, q_count)

        def tile_output(q_start=q_start, q_count=q_count, live_mask=live_mask):
            scores = tile_scores(key_block)
            weights = jnp.where(
                live_mask[None],
                jnp.exp(scores - log_sum[:, q_start : q_start + q_count, None]),
                0.0,
            )
            probs = weights.astype(jnp.bfloat16)
            return jnp.einsum("hrk,kd->rhd", probs, value_block, preferred_element_type=jnp.float32)

        out_acc = out_acc.at[q_start : q_start + q_count].add(tile_output())
        return out_acc

    out_acc = sweep(add_output, jnp.zeros((tok_dev, head_count, head_width), jnp.float32))
    attention = out_acc.astype(jnp.bfloat16)
    delta = jnp.sum(cotangent.astype(jnp.float32) * attention.astype(jnp.float32), axis=2).T

    def grads_of(grad_q_acc, kv_block, k_place, k_docs):
        key_block = kv_block[:, :head_width]
        value_block = kv_block[:, head_width:]
        q_start, q_count = q_spans[0]
        live_mask = live_pairs(k_place, k_docs, q_start, q_count)

        def tile_grads(q_start=q_start, q_count=q_count, live_mask=live_mask):
            scores = tile_scores(key_block)
            weights = jnp.where(
                live_mask[None],
                jnp.exp(scores - log_sum[:, q_start : q_start + q_count, None]),
                0.0,
            )
            probs = weights.astype(jnp.bfloat16)
            dprobs = jnp.einsum(
                "rhd,kd->hrk", cotangent, value_block, preferred_element_type=jnp.float32
            )
            dscores = (
                weights * (dprobs - delta[:, q_start : q_start + q_count, None]) * score_scale
            ).astype(jnp.bfloat16)
            q_part = jnp.einsum(
                "hrk,kd->rhd", dscores, key_block, preferred_element_type=jnp.float32
            )
            k_part = jnp.einsum("hrk,rhd->kd", dscores, queries, preferred_element_type=jnp.float32)
            v_part = jnp.einsum("hrk,rhd->kd", probs, cotangent, preferred_element_type=jnp.float32)
            return (q_part, jnp.concatenate([k_part, v_part], axis=1))

        q_part, tile_part = tile_grads()
        grad_q_acc = grad_q_acc.at[q_start : q_start + q_count].add(q_part)
        return (grad_q_acc, tile_part)

    grad_q_acc, own_part = grads_of(
        jnp.zeros((tok_dev, head_count, head_width), jnp.float32), packed, q_place, q_docs
    )

    def back_step(carried, step_index):
        grad_q_acc, kv_lower, kv_upper = carried
        kv_lower = from_behind(kv_lower, "ctx", 1)
        kv_upper = from_behind(kv_upper, "ctx", -1)
        k_place, k_docs = positions((my_index - step_index) * tok_dev, tok_dev)
        grad_q_acc, lower_part = grads_of(grad_q_acc, kv_lower, k_place, k_docs)
        k_place, k_docs = positions((my_index + step_index) * tok_dev, tok_dev)
        grad_q_acc, upper_part = grads_of(grad_q_acc, kv_upper, k_place, k_docs)
        return ((grad_q_acc, kv_lower, kv_upper), (lower_part, upper_part))

    (grad_q_acc, kv_lower, kv_upper), (lower_parts, upper_parts) = lax.scan(
        back_step, (grad_q_acc, packed, packed), jnp.arange(1, reach_count + 1, dtype=jnp.int32)
    )
    from_lower = fold_home(lower_parts, False)
    from_upper = fold_home(upper_parts, True)
    kv_total = own_part + from_lower + from_upper
    kv_total = lax.psum(kv_total.astype(jnp.bfloat16), "head").astype(jnp.float32)
    kv_grads = kv_total.astype(jnp.bfloat16)
    attention_out = attention.reshape(tok_dev, head_count * head_width)
    grad_query = grad_q_acc.astype(jnp.bfloat16).reshape(tok_dev, head_count * head_width)
    return (attention_out, grad_query, kv_grads[:, :head_width], kv_grads[:, head_width:])


def solution(mesh):
    in_specs = (P("ctx", "head"), P("ctx", None), P("ctx", None), P("ctx", "head"), P())
    out_specs = (P("ctx", "head"), P("ctx", "head"), P("ctx", None), P("ctx", None))
    return jax.shard_map(body, mesh=mesh, in_specs=in_specs, out_specs=out_specs, check_vma=False)
```

profile of v0, /device:TPU:0, one launch (start us, length us, event | category | flops | bytes accessed | tf_op | source)
XLA Modules:
  0.0 74.6 jit_solution(12013771210908291032)
XLA Ops:
  7.2 0.0 copy-start.1
  7.2 0.0 copy-start.2
  7.2 0.0 all-reduce.4.cloned.1.call-start
  7.2 0.8 %constant_dynamic-update-slice_fusion.1 = bf16[128,256]{1,0:T(8,128)(2,1)S(1)} fusion(bf16[128,128]{1,0:T(8,128)(2,1)} %param.72), kind=kLoop, calls=%fused_computation.78 | loop fusion | bytes 65536
  8.0 0.0 copy-done.1
  8.1 1.3 %collective-permute-start.1 = (bf16[128,256]{1,0:T(8,128)(2,1)S(1)}, bf16[128,256]{1,0:T(8,128)(2,1)S(1)}, u32[]{:S(2)}, u32[]{:S(2)}) collective-permute-start(bf16[128,256]{1,0:T(8,128)(2,1)S(1)} %constant_dynamic-update-slice_fusion), channel_id=1, source_target_pairs={{4,0},{8,4},{12,8},{16,12},{20,16},{24,20},{28,24},{5,1},{9,5},{13... | collective-permute-start | bytes 196616 | tf_op jit(solution)/shard_map/while/body/eval_jaxpr/ppermute | solution.py:11
  9.4 5.5 %collective-permute-start = (bf16[128,256]{1,0:T(8,128)(2,1)S(1)}, bf16[128,256]{1,0:T(8,128)(2,1)S(1)}, u32[]{:S(2)}, u32[]{:S(2)}) collective-permute-start(bf16[128,256]{1,0:T(8,128)(2,1)S(1)} %constant_dynamic-update-slice_fusion), channel_id=1, source_target_pairs={{0,4},{4,8},{8,12},{12,16},{16,20},{20,24},{24,28},{1,5},{5,9},{9,... | collective-permute-start | bytes 196616 | tf_op jit(solution)/shard_map/while/body/eval_jaxpr/ppermute | solution.py:11
  15.0 0.7 copy.85
  15.7 0.1 reduce-window.8
  15.8 0.1 reduce.58
  15.9 0.0 copy-done.2
  15.9 0.0 copy-start.3
  15.9 0.1 copy.95
  16.0 0.8 %copy-done.3 = bf16[128,512]{1,0:T(8,128)(2,1)S(1)} copy-done((bf16[128,512]{1,0:T(8,128)(2,1)S(1)}, bf16[128,512]{1,0:T(8,128)(2,1)}, u32[]{:S(2)}) %copy-start.3) | copy-done | bytes 131096
  16.8 0.1 copy.145
  16.9 0.1 convert_reduce_fusion.1
  17.0 0.0 copy-start
  17.0 0.2 and_and_fusion.1
  17.2 0.5 copy-done
  17.8 0.2 select_reduce_fusion.5
  17.9 0.1 select_reduce_fusion.2
  18.0 0.0 collective-permute-done.1
  18.0 0.2 select_reduce_fusion.3
  18.2 0.1 select_reduce_fusion
  18.3 0.0 collective-permute-done
  18.3 0.2 select_reduce_fusion.4
  18.5 0.1 select_reduce_fusion.1
  18.6 0.2 convolution_bitcast_fusion.11
  18.8 0.2 convolution_bitcast_fusion.9
  19.0 0.2 convolution_bitcast_fusion.13
  19.2 0.2 convolution_bitcast_fusion.8
  19.5 0.2 fusion.15
  19.7 0.2 multiply_reduce_fusion
  19.9 0.2 fusion.17
  20.1 0.2 fusion.18
  20.3 0.2 convolution_bitcast_fusion.12
  20.5 0.2 fusion.19
  20.7 0.2 convolution_bitcast_fusion.10
  21.0 0.2 convolution_bitcast_fusion.14
  21.1 0.2 convolution_bitcast_fusion.4
  21.4 4.8 %collective-permute-start.3 = (bf16[1,128,256]{1,2,0:T(8,128)(2,1)S(1)}, bf16[1,128,256]{1,2,0:T(8,128)(2,1)S(1)}, u32[]{:S(2)}, u32[]{:S(2)}) collective-permute-start(bf16[1,128,256]{1,2,0:T(8,128)(2,1)S(1)} %fusion.65), channel_id=1, source_target_pairs={{0,4},{4,8},{8,12},{12,16},{16,20},{20,24},{24,28},{1,5},{5,9},{9,... | collective-permute-start | bytes 196616 | tf_op jit(solution)/shard_map/ppermute | solution.py:11
  26.2 1.3 %collective-permute-start.2 = (bf16[1,128,256]{1,2,0:T(8,128)(2,1)S(1)}, bf16[1,128,256]{1,2,0:T(8,128)(2,1)S(1)}, u32[]{:S(2)}, u32[]{:S(2)}) collective-permute-start(bf16[1,128,256]{1,2,0:T(8,128)(2,1)S(1)} %fusion.66), channel_id=1, source_target_pairs={{4,0},{8,4},{12,8},{16,12},{20,16},{24,20},{28,24},{5,1},{9,5},{13... | collective-permute-start | bytes 196616 | tf_op jit(solution)/shard_map/ppermute | solution.py:11
  27.6 0.2 fusion.7
  27.8 0.3 collective-permute-done.3
  28.1 4.3 %collective-permute-done.2 = bf16[1,128,256]{1,2,0:T(8,128)(2,1)S(1)} collective-permute-done((bf16[1,128,256]{1,2,0:T(8,128)(2,1)S(1)}, bf16[1,128,256]{1,2,0:T(8,128)(2,1)S(1)}, u32[]{:S(2)}, u32[]{:S(2)}) %collective-permute-start.2) | collective-permute-done | bytes 65568 | tf_op jit(solution)/shard_map/ppermute | solution.py:11
  32.4 0.7 fusion.26
  33.0 0.0 all-reduce.4.cloned.1.call-update
  33.0 0.2 fusion.20
  33.3 0.8 %copy.114 = bf16[128,512]{1,0:T(8,128)(2,1)} copy(bf16[128,512]{0,1:T(8,128)(2,1)S(1)} %bitcast.169) | data formatting | bytes 262144
  34.0 0.8 %copy.115 = bf16[128,512]{1,0:T(8,128)(2,1)} copy(bf16[128,512]{0,1:T(8,128)(2,1)S(1)} %bitcast.170) | data formatting | bytes 262144
  34.8 30.8 %all-reduce.4.cloned.1.call-done = bf16[128,256]{0,1:T(8,128)(2,1)} async-done(((bf16[128,256]{0,1:T(8,128)(2,1)}), bf16[128,256]{0,1:T(8,128)(2,1)}) %all-reduce.4.cloned.1.call-update) | async-done | bytes 65552 | tf_op jit(solution)/shard_map/psum | solution.py:198
  65.6 0.8 %fusion.67 = (bf16[128,128]{0,1:T(8,128)(2,1)S(1)}, bf16[128,128]{0,1:T(8,128)(2,1)S(1)}) fusion(bf16[128,256]{0,1:T(8,128)(2,1)} %all-reduce.4.cloned.1.call-done), kind=kLoop, calls=%fused_computation.149 | loop fusion | bytes 131072 | tf_op jit(solution)/shard_map/slice | solution.py:202
  66.3 0.7 copy.117
  67.1 0.7 copy.116
  (14 shorter events, 0.2 us)
Async XLA Ops:
  7.2 0.9 %copy-start.1 = (bf16[128,128]{1,0:T(8,128)(2,1)S(1)}, bf16[128,128]{1,0:T(8,128)(2,1)}, u32[]{:S(2)}) copy-start(bf16[128,128]{1,0:T(8,128)(2,1)} %param.73) | copy-start | bytes 98308
  7.2 8.7 %copy-start.2 = (bf16[128,512]{1,0:T(8,128)(2,1)S(1)}, bf16[128,512]{1,0:T(8,128)(2,1)}, u32[]{:S(2)}) copy-start(bf16[128,512]{1,0:T(8,128)(2,1)} %param.74) | copy-start | bytes 393220
  7.2 58.4 %all-reduce.4.cloned.1.call-start = ((), (), s32[]{:S(2)}) async-start(), calls=%async_computation | async-start | bytes 131072 | tf_op jit(solution)/shard_map/psum | solution.py:198
  8.1 10.0 %collective-permute-start.1 = (bf16[128,256]{1,0:T(8,128)(2,1)S(1)}, bf16[128,256]{1,0:T(8,128)(2,1)S(1)}, u32[]{:S(2)}, u32[]{:S(2)}) collective-permute-start(bf16[128,256]{1,0:T(8,128)(2,1)S(1)} %constant_dynamic-update-slice_fusion), channel_id=1, source_target_pairs={{4,0},{8,4},{12,8},{16,12},{20,16},{24,20},{28,24},{5,1},{9,5},{13... | collective-permute-start | bytes 196616 | tf_op jit(solution)/shard_map/while/body/eval_jaxpr/ppermute | solution.py:11
  9.4 8.9 %collective-permute-start = (bf16[128,256]{1,0:T(8,128)(2,1)S(1)}, bf16[128,256]{1,0:T(8,128)(2,1)S(1)}, u32[]{:S(2)}, u32[]{:S(2)}) collective-permute-start(bf16[128,256]{1,0:T(8,128)(2,1)S(1)} %constant_dynamic-update-slice_fusion), channel_id=1, source_target_pairs={{0,4},{4,8},{8,12},{12,16},{16,20},{20,24},{24,28},{1,5},{5,9},{9,... | collective-permute-start | bytes 196616 | tf_op jit(solution)/shard_map/while/body/eval_jaxpr/ppermute | solution.py:11
  15.9 0.9 %copy-start.3 = (bf16[128,512]{1,0:T(8,128)(2,1)S(1)}, bf16[128,512]{1,0:T(8,128)(2,1)}, u32[]{:S(2)}) copy-start(bf16[128,512]{1,0:T(8,128)(2,1)} %param.71) | copy-start | bytes 393220
  17.0 0.8 %copy-start = (bf16[128,128]{1,0:T(8,128)(2,1)S(1)}, bf16[128,128]{1,0:T(8,128)(2,1)}, u32[]{:S(2)}) copy-start(bf16[128,128]{1,0:T(8,128)(2,1)} %param.72) | copy-start | bytes 98308
  21.4 6.7 %collective-permute-start.3 = (bf16[1,128,256]{1,2,0:T(8,128)(2,1)S(1)}, bf16[1,128,256]{1,2,0:T(8,128)(2,1)S(1)}, u32[]{:S(2)}, u32[]{:S(2)}) collective-permute-start(bf16[1,128,256]{1,2,0:T(8,128)(2,1)S(1)} %fusion.65), channel_id=1, source_target_pairs={{0,4},{4,8},{8,12},{12,16},{16,20},{20,24},{24,28},{1,5},{5,9},{9,... | collective-permute-start | bytes 196616 | tf_op jit(solution)/shard_map/ppermute | solution.py:11
  26.2 6.2 %collective-permute-start.2 = (bf16[1,128,256]{1,2,0:T(8,128)(2,1)S(1)}, bf16[1,128,256]{1,2,0:T(8,128)(2,1)S(1)}, u32[]{:S(2)}, u32[]{:S(2)}) collective-permute-start(bf16[1,128,256]{1,2,0:T(8,128)(2,1)S(1)} %fusion.66), channel_id=1, source_target_pairs={{4,0},{8,4},{12,8},{16,12},{20,16},{24,20},{28,24},{5,1},{9,5},{13... | collective-permute-start | bytes 196616 | tf_op jit(solution)/shard_map/ppermute | solution.py:11
Sparse Core Ops, SparseCore 0:
  33.2 32.3 all-reduce.3
where the time goes:
time: 75 us; the launch traced here: 74.6 us
  waiting for transfers between devices  35.3 us (47%)
  between operations  14.4 us (19%)
  starting transfers between devices  12.9 us (17%)
  local copies, waits for them, and re-layouts  6.92 us (9%)
  matrix products  3.6 us (5%)
  other arithmetic  1.5 us (2%)
    psum x1, waiting for transfers between devices, body(): lax.psum(kv_total.astype(jnp.bfloat16), 'head').astype(jnp.float32)  30.8 us
    ppermute x4, starting transfers between devices, from_behind(): return lax.ppermute(array, axis, pairs)  12.9 us
    unnamed x14, local copies, waits for them, and re-layouts  5.21 us
    ppermute x4, waiting for transfers between devices, from_behind(): return lax.ppermute(array, axis, pairs)  4.55 us
  transfers between devices with their start and end apart: 5, of which 3 were waited for; matrix products, arithmetic and copies ran while one was open for 5% of the time, Pallas kernels for 0%

commit v1 on v0

--- a/solution.py
+++ b/solution.py
@@ -1,7 +1,10 @@
+import functools
+
 import jax
 import jax.numpy as jnp
-import numpy as np
 from jax import lax
+from jax.experimental import pallas as pl
+from jax.experimental.pallas import tpu as pltpu
 from jax.sharding import PartitionSpec as P
 
 
@@ -13,22 +16,17 @@
 
 def fold_home(key_parts, upward):
     slot_count = key_parts.shape[0]
-    slot_grads = jnp.concatenate(
-        [jnp.zeros((1,) + key_parts.shape[1:], jnp.float32), key_parts], axis=0
-    )
+    slots = [jnp.zeros(key_parts.shape[1:], jnp.float32)]
+    slots += [key_parts[i] for i in range(slot_count)]
     for bit_index in range(slot_count.bit_length()):
         offset = 1 << bit_index
-        moving_slots = np.array(
-            [slot for slot in range(slot_count + 1) if slot & offset], dtype=np.int32
-        )
-        moving = slot_grads[moving_slots]
-        if upward:
-            arrived = from_behind(moving.astype(jnp.bfloat16), "ctx", offset).astype(moving.dtype)
-        else:
-            arrived = from_behind(moving.astype(jnp.bfloat16), "ctx", -offset).astype(moving.dtype)
-        slot_grads = slot_grads.at[moving_slots].set(0.0)
-        slot_grads = slot_grads.at[moving_slots - offset].add(arrived)
-    return slot_grads[0]
+        moving = [slot for slot in range(slot_count + 1) if slot & offset]
+        sent = jnp.stack([slots[slot] for slot in moving]).astype(jnp.bfloat16)
+        arrived = from_behind(sent, "ctx", offset if upward else -offset).astype(jnp.float32)
+        for i, slot in enumerate(moving):
+            slots[slot] = jnp.zeros_like(slots[slot])
+            slots[slot - offset] = slots[slot - offset] + arrived[i]
+    return slots[0]
 
 
 def body(query, key, value, grad_out, doc_lengths):
@@ -40,7 +38,8 @@
     n_context = lax.axis_size("ctx")
     reach_count = n_context // 8
     my_index = lax.axis_index("ctx")
-    doc_ends = jnp.cumsum(doc_lengths)
+    docs = jnp.arange(doc_lengths.shape[0])
+    doc_ends = jnp.sum(jnp.where(docs[None, :] <= docs[:, None], doc_lengths[None, :], 0), axis=1)
 
     def positions(first_row, row_count):
         global_row = first_row + jnp.arange(row_count, dtype=jnp.int32)
@@ -202,7 +201,354 @@
     return (attention_out, grad_query, kv_grads[:, :head_width], kv_grads[:, head_width:])
 
 
+MESH = pl.DeviceIdType.MESH
+NT = (((1,), (1,)), ((), ()))
+TN = (((0,), (0,)), ((), ()))
+NN = (((1,), (0,)), ((), ()))
+
+
+def dot(lhs, rhs, dims):
+    return lax.dot_general(lhs, rhs, dims, preferred_element_type=jnp.float32)
+
+
+def near_kernel(
+    n_ctx,
+    n_head,
+    lens_ref,
+    q_hbm,
+    k_hbm,
+    v_hbm,
+    g_hbm,
+    o_ref,
+    dq_ref,
+    dk_ref,
+    dv_ref,
+    q_ref,
+    g_ref,
+    kv_ref,
+    halo_ref,
+    own_part,
+    own_send,
+    halo_send,
+    own_recv,
+    halo_recv,
+    final,
+    load_sem,
+    kv_send_sem,
+    kv_recv_sem,
+    own_send_sem,
+    own_recv_sem,
+    hs_send_sem,
+    hs_recv_sem,
+    fin_send_sem,
+    fin_recv_sem,
+):
+    c = lax.axis_index("ctx")
+    h = lax.axis_index("head")
+    width = k_hbm.shape[1]
+    tok = k_hbm.shape[0]
+    st = tok // 2
+    heads = q_hbm.shape[1] // width
+    rows = heads * st
+    quarter = tok // n_head
+    per_half = n_head // 2
+    has_prev = c > 0
+    has_next = c < n_ctx - 1
+
+    barrier = pltpu.get_barrier_semaphore()
+    for d in range(1, n_head):
+        pl.semaphore_signal(
+            barrier, inc=1, device_id=(c, lax.rem(h + d, n_head)), device_id_type=MESH
+        )
+
+    @pl.when(has_prev)
+    def _():
+        for d in range(n_head):
+            pl.semaphore_signal(barrier, inc=1, device_id=(c - 1, d), device_id_type=MESH)
+
+    @pl.when(has_next)
+    def _():
+        for d in range(n_head):
+            pl.semaphore_signal(barrier, inc=1, device_id=(c + 1, d), device_id_type=MESH)
+
+    loads = [
+        pltpu.make_async_copy(k_hbm, kv_ref.at[:, pl.ds(0, width)], load_sem.at[0]),
+        pltpu.make_async_copy(v_hbm, kv_ref.at[:, pl.ds(width, width)], load_sem.at[1]),
+        pltpu.make_async_copy(q_hbm, q_ref, load_sem.at[2]),
+        pltpu.make_async_copy(g_hbm, g_ref, load_sem.at[3]),
+    ]
+    for load in loads:
+        load.start()
+
+    lane = lax.broadcasted_iota(jnp.int32, (1, rows), 1)
+    place = lax.rem(lane, st)
+    key_row = lax.broadcasted_iota(jnp.int32, (2 * st, rows), 0)
+    bases = (c * st, (2 * n_ctx - 1 - c) * st)
+    starts = [jnp.zeros((1, rows), jnp.int32) for _ in bases]
+    doc_end = jnp.int32(0)
+    for doc in range(lens_ref.shape[0]):
+        doc_end = doc_end + lens_ref[doc]
+        for i, base in enumerate(bases):
+            starts[i] = jnp.where(place + base >= doc_end, doc_end, starts[i])
+    live = [
+        (key_row + (base - st) >= start) & (key_row - st <= place)
+        for base, start in zip(bases, starts)
+    ]
+
+    loads[0].wait()
+    loads[1].wait()
+    pl.semaphore_wait(
+        barrier,
+        (n_head - 1) + n_head * has_prev.astype(jnp.int32) + n_head * has_next.astype(jnp.int32),
+    )
+
+    def kv_copy(part, step):
+        return pltpu.make_async_remote_copy(
+            src_ref=kv_ref.at[pl.ds(part * st, st), :],
+            dst_ref=halo_ref.at[part],
+            send_sem=kv_send_sem.at[part],
+            recv_sem=kv_recv_sem.at[part],
+            device_id=(c + step, h),
+            device_id_type=MESH,
+        )
+
+    lower_kv, upper_kv = kv_copy(0, 1), kv_copy(1, -1)
+
+    @pl.when(has_next)
+    def _():
+        lower_kv.start()
+
+    @pl.when(has_prev)
+    def _():
+        upper_kv.start()
+
+    loads[2].wait()
+    loads[3].wait()
+
+    def stacked(ref, part):
+        return jnp.concatenate(
+            [
+                ref[part * st : (part + 1) * st, i * width : (i + 1) * width]
+                for i in range(heads)
+            ],
+            axis=0,
+        )
+
+    qs = [stacked(q_ref, part) for part in range(2)]
+    gs = [stacked(g_ref, part) for part in range(2)]
+    k_own = [kv_ref[part * st : (part + 1) * st, :width] for part in range(2)]
+    v_own = [kv_ref[part * st : (part + 1) * st, width:] for part in range(2)]
+    s_own = [dot(k_own[part], qs[part], NT) for part in range(2)]
+    dp_own = [dot(v_own[part], gs[part], NT) for part in range(2)]
+
+    @pl.when(has_prev)
+    def _():
+        lower_kv.wait_recv()
+
+    @pl.when(has_next)
+    def _():
+        upper_kv.wait_recv()
+
+    zero = jnp.zeros((st, 2 * width), jnp.bfloat16)
+    halos = [
+        jnp.where(has_prev, halo_ref[0], zero),
+        jnp.where(has_next, halo_ref[1], kv_ref[0:st, :]),
+    ]
+    scale = width ** (-0.5)
+    probs, dscores, keys, values, grads = [], [], [], [], []
+    for part in range(2):
+        k_halo, v_halo = halos[part][:, :width], halos[part][:, width:]
+        scores = jnp.concatenate([dot(k_halo, qs[part], NT), s_own[part]], axis=0) * scale
+        dprobs = jnp.concatenate([dot(v_halo, gs[part], NT), dp_own[part]], axis=0)
+        scores = jnp.where(live[part], scores, -1e30)
+        peak = jnp.max(scores, axis=0, keepdims=True)
+        raw = jnp.where(live[part], jnp.exp(scores - peak), 0.0)
+        weights = raw * (1.0 / jnp.sum(raw, axis=0, keepdims=True))
+        prob = weights.astype(jnp.bfloat16)
+        delta = jnp.sum(prob.astype(jnp.float32) * dprobs, axis=0, keepdims=True)
+        dscore = (weights * (dprobs - delta) * scale).astype(jnp.bfloat16)
+        grad_k = dot(dscore, qs[part], NN)
+        grad_v = dot(prob, gs[part], NN)
+        probs.append(prob)
+        dscores.append(dscore)
+        keys.append(jnp.concatenate([k_halo, k_own[part]], axis=0))
+        values.append(jnp.concatenate([v_halo, v_own[part]], axis=0))
+        grads.append(jnp.concatenate([grad_k, grad_v], axis=1))
+
+    lower = grads[0][st:] + jnp.where(has_next, 0.0, grads[1][:st])
+    own_part[0:st, :] = lower
+    own_part[st:tok, :] = grads[1][st:]
+    own_send[0:st, :] = lower.astype(jnp.bfloat16)
+    own_send[st:tok, :] = grads[1][st:].astype(jnp.bfloat16)
+    halo_send[0] = grads[0][:st].astype(jnp.bfloat16)
+    halo_send[1] = grads[1][:st].astype(jnp.bfloat16)
+
+    def halo_copy(part, j, step):
+        return pltpu.make_async_remote_copy(
+            src_ref=halo_send.at[part, pl.ds(j * quarter, quarter), :],
+            dst_ref=halo_recv.at[h],
+            send_sem=hs_send_sem.at[part, j],
+            recv_sem=hs_recv_sem.at[h],
+            device_id=(c + step, part * per_half + j),
+            device_id_type=MESH,
+        )
+
+    down = [halo_copy(0, j, -1) for j in range(per_half)]
+    up = [halo_copy(1, j, 1) for j in range(per_half)]
+
+    @pl.when(has_prev)
+    def _():
+        for copy in down:
+            copy.start()
+
+    @pl.when(has_next)
+    def _():
+        for copy in up:
+            copy.start()
+
+    own_copies = []
+    for d in range(1, n_head):
+        peer = lax.rem(h + d, n_head)
+        own_copies.append(
+            pltpu.make_async_remote_copy(
+                src_ref=own_send.at[pl.ds(pl.multiple_of(peer * quarter, quarter), quarter), :],
+                dst_ref=own_recv.at[d - 1],
+                send_sem=own_send_sem.at[d - 1],
+                recv_sem=own_recv_sem.at[d - 1],
+                device_id=(c, peer),
+                device_id_type=MESH,
+            )
+        )
+    for copy in own_copies:
+        copy.start()
+
+    for part in range(2):
+        out = dot(probs[part], values[part], TN).astype(jnp.bfloat16)
+        grad_q = dot(dscores[part], keys[part], TN).astype(jnp.bfloat16)
+        for i in range(heads):
+            where = (slice(part * st, (part + 1) * st), slice(i * width, (i + 1) * width))
+            o_ref[where] = out[i * st : (i + 1) * st]
+            dq_ref[where] = grad_q[i * st : (i + 1) * st]
+
+    mine = pl.ds(pl.multiple_of(h * quarter, quarter), quarter)
+    gets_halo = jnp.where(h < per_half, has_next.astype(jnp.int32), has_prev.astype(jnp.int32))
+
+    @pl.when(gets_halo == 1)
+    def _():
+        for j in range(n_head):
+            pltpu.make_async_remote_copy(
+                src_ref=halo_recv.at[j],
+                dst_ref=halo_recv.at[j],
+                send_sem=hs_send_sem.at[0, 0],
+                recv_sem=hs_recv_sem.at[j],
+                device_id=(c, lax.rem(h + 1, n_head)),
+                device_id_type=MESH,
+            ).wait_recv()
+
+    total = own_part[mine, :]
+    for d in range(n_head - 1):
+        own_copies[d].wait_recv()
+        total = total + own_recv[d].astype(jnp.float32)
+    near = halo_recv[0].astype(jnp.float32)
+    for j in range(1, n_head):
+        near = near + halo_recv[j].astype(jnp.float32)
+    total = total + jnp.where(gets_halo == 1, near, 0.0)
+    final[mine, :] = total.astype(jnp.bfloat16)
+
+    fin_copies = []
+    for d in range(1, n_head):
+        fin_copies.append(
+            pltpu.make_async_remote_copy(
+                src_ref=final.at[mine, :],
+                dst_ref=final.at[mine, :],
+                send_sem=fin_send_sem.at[d - 1],
+                recv_sem=fin_recv_sem.at[d - 1],
+                device_id=(c, lax.rem(h + d, n_head)),
+                device_id_type=MESH,
+            )
+        )
+    for copy in fin_copies:
+        copy.start()
+
+    @pl.when(has_next)
+    def _():
+        lower_kv.wait_send()
+        for copy in up:
+            copy.wait_send()
+
+    @pl.when(has_prev)
+    def _():
+        upper_kv.wait_send()
+        for copy in down:
+            copy.wait_send()
+
+    for copy in own_copies:
+        copy.wait_send()
+    for d in range(1, n_head):
+        sender = lax.rem(h + n_head - d, n_head)
+        theirs = pl.ds(pl.multiple_of(sender * quarter, quarter), quarter)
+        pltpu.make_async_remote_copy(
+            src_ref=final.at[theirs, :],
+            dst_ref=final.at[theirs, :],
+            send_sem=fin_send_sem.at[d - 1],
+            recv_sem=fin_recv_sem.at[d - 1],
+            device_id=(c, lax.rem(h + d, n_head)),
+            device_id_type=MESH,
+        ).wait_recv()
+    dk_ref[...] = final[:, :width]
+    dv_ref[...] = final[:, width:]
+    for copy in fin_copies:
+        copy.wait_send()
+
+
+def near_body(n_ctx, n_head, query, key, value, grad_out, doc_lengths):
+    tok, width = key.shape
+    st = tok // 2
+    quarter = tok // n_head
+    bf16, f32 = jnp.bfloat16, jnp.float32
+    dma = pltpu.SemaphoreType.DMA
+    vmem = pl.BlockSpec(memory_space=pltpu.VMEM)
+    hbm = pl.BlockSpec(memory_space=pl.ANY)
+    return pl.pallas_call(
+        functools.partial(near_kernel, n_ctx, n_head),
+        out_shape=(
+            jax.ShapeDtypeStruct(query.shape, bf16),
+            jax.ShapeDtypeStruct(query.shape, bf16),
+            jax.ShapeDtypeStruct(key.shape, bf16),
+            jax.ShapeDtypeStruct(key.shape, bf16),
+        ),
+        in_specs=[pl.BlockSpec(memory_space=pltpu.SMEM), hbm, hbm, hbm, hbm],
+        out_specs=(vmem, vmem, vmem, vmem),
+        scratch_shapes=[
+            pltpu.VMEM(query.shape, bf16),
+            pltpu.VMEM(query.shape, bf16),
+            pltpu.VMEM((tok, 2 * width), bf16),
+            pltpu.VMEM((2, st, 2 * width), bf16),
+            pltpu.VMEM((tok, 2 * width), f32),
+            pltpu.VMEM((tok, 2 * width), bf16),
+            pltpu.VMEM((2, st, 2 * width), bf16),
+            pltpu.VMEM((n_head - 1, quarter, 2 * width), bf16),
+            pltpu.VMEM((n_head, quarter, 2 * width), bf16),
+            pltpu.VMEM((tok, 2 * width), bf16),
+            dma((4,)),
+            dma((2,)),
+            dma((2,)),
+            dma((n_head - 1,)),
+            dma((n_head - 1,)),
+            dma((2, n_head // 2)),
+            dma((n_head,)),
+            dma((n_head - 1,)),
+            dma((n_head - 1,)),
+        ],
+        compiler_params=pltpu.CompilerParams(
+            collective_id=0, has_side_effects=True, vmem_limit_bytes=16 * 1024 * 1024
+        ),
+    )(doc_lengths, query, key, value, grad_out)
+
+
 def solution(mesh):
     in_specs = (P("ctx", "head"), P("ctx", None), P("ctx", None), P("ctx", "head"), P())
     out_specs = (P("ctx", "head"), P("ctx", "head"), P("ctx", None), P("ctx", None))
-    return jax.shard_map(body, mesh=mesh, in_specs=in_specs, out_specs=out_specs, check_vma=False)
+    n_ctx, n_head = mesh.shape["ctx"], mesh.shape["head"]
+    run = functools.partial(near_body, n_ctx, n_head) if n_ctx // 8 == 1 else body
+    return jax.shard_map(run, mesh=mesh, in_specs=in_specs, out_specs=out_specs, check_vma=False)

time: 75 us -> 21.8 us (0.29)
  waiting for transfers between devices: 35.3 us -> 0 us
  Pallas kernels: 0 us -> 14.4 us
  between operations: 14.4 us -> 0.65 us
  starting transfers between devices: 12.9 us -> 0 us
  matrix products: 3.6 us -> 0 us
  other arithmetic: 1.5 us -> 0 us
    psum x1 -> x0, waiting for transfers between devices: 30.8 us -> none  [body(): lax.psum(kv_total.astype(jnp.bfloat16), 'head').astype(jnp.float32)]
    pallas_call x0 -> x1, Pallas kernels: none -> 14.4 us  [near_body(): pl.pallas_call(functools.partial(near_kernel, n_ctx, n_head), out_shape=(...]
    ppermute x4 -> x0, starting transfers between devices: 12.9 us -> none  [from_behind(): return lax.ppermute(array, axis, pairs)]
    ppermute x4 -> x0, waiting for transfers between devices: 4.55 us -> none  [from_behind(): return lax.ppermute(array, axis, pairs)]
    dot_general x18 -> x0, matrix products: 3.6 us -> none  [the longest x3 0.66 us: tile_output(): jnp.einsum('hrk,kd->rhd', probs, value_block, preferred_element_type=jnp....]
    unnamed x14, local copies, waits for them, and re-layouts: 5.21 us -> 6.51 us
    slice x1 -> x0, local copies, waits for them, and re-layouts: 0.78 us -> none  [body(): kv_grads[:, head_width:]]
  transfers between devices with their start and end apart: 5 -> 0, of which waited for: 3 -> 0; matrix products, arithmetic and copies ran while one was open for 5% -> 0% of each run, Pallas kernels for 0% -> 0%
where the time goes in v1:
time: 21.8 us; the launch traced here: 21.5 us
  Pallas kernels  14.4 us (66%)
  local copies, waits for them, and re-layouts  6.51 us (30%)
  between operations  0.65 us (3%)
    pallas_call x1, Pallas kernels, near_body(): pl.pallas_call(functools.partial(near_kernel, n_ctx, n_head), out_shape=(...  14.4 us
    unnamed x14, local copies, waits for them, and re-layouts  6.51 us

profile of v1, /device:TPU:0, one launch (start us, length us, event | category | flops | bytes accessed | tf_op | source)
XLA Modules:
  0.0 21.5 jit_solution(2503379619729390575)
XLA Ops:
  0.6 0.0 copy-start
  0.6 0.9 %copy-done = bf16[128,512]{1,0:T(8,128)(2,1)S(1)} copy-done((bf16[128,512]{1,0:T(8,128)(2,1)S(1)}, bf16[128,512]{1,0:T(8,128)(2,1)}, u32[]{:S(2)}) %copy-start) | copy-done | bytes 131096
  1.5 0.0 copy-start.1
  1.5 0.9 %copy-done.1 = bf16[128,512]{1,0:T(8,128)(2,1)S(1)} copy-done((bf16[128,512]{1,0:T(8,128)(2,1)S(1)}, bf16[128,512]{1,0:T(8,128)(2,1)}, u32[]{:S(2)}) %copy-start.1) | copy-done | bytes 131096
  2.4 0.0 copy-start.2
  2.4 0.8 %copy-done.2 = bf16[128,128]{1,0:T(8,128)(2,1)S(1)} copy-done((bf16[128,128]{1,0:T(8,128)(2,1)S(1)}, bf16[128,128]{1,0:T(8,128)(2,1)}, u32[]{:S(2)}) %copy-start.2) | copy-done | bytes 32792
  3.2 0.0 copy-start.3
  3.2 0.8 %copy-done.3 = bf16[128,128]{1,0:T(8,128)(2,1)S(1)} copy-done((bf16[128,128]{1,0:T(8,128)(2,1)S(1)}, bf16[128,128]{1,0:T(8,128)(2,1)}, u32[]{:S(2)}) %copy-start.3) | copy-done | bytes 32792
  4.0 0.0 copy-start.4
  4.0 0.7 %copy-done.4 = s32[32]{0:T(128)S(1)} copy-done((s32[32]{0:T(128)S(1)}, s32[32]{0:T(128)}, u32[]{:S(2)}) %copy-start.4) | copy-done | bytes 152
  4.6 14.4 %shard_map.84 = (bf16[128,512]{1,0:T(8,128)(2,1)S(1)}, bf16[128,512]{1,0:T(8,128)(2,1)S(1)}, bf16[128,128]{1,0:T(8,128)(2,1)S(1)}, bf16[128,128]{1,0:T(8,128)(2,1)S(1)}) custom-call(s32[32]{0:T(128)S(1)} %copy-done.4, bf16[128,512]{1,0:T(8,128)(2,1)S(1)} %copy-done, bf16[128,128]{1,0:T(8,128)(2,1)S(1)} %copy-done.2, bf16[128,128]{1,0:T(8,128)(2,1)S(1)} %copy-done.3, ...), custom_call_target="tpu_custom_call" | custom-call | tf_op jit(solution)/shard_map/pallas_call | solution.py:512
  19.0 0.7 %copy.13 = bf16[128,512]{1,0:T(8,128)(2,1)} copy(bf16[128,512]{1,0:T(8,128)(2,1)S(1)} %get-tuple-element.8) | data formatting | bytes 262144
  19.7 0.7 %copy.14 = bf16[128,512]{1,0:T(8,128)(2,1)} copy(bf16[128,512]{1,0:T(8,128)(2,1)S(1)} %get-tuple-element.9) | data formatting | bytes 262144
  20.3 0.6 %copy.15 = bf16[128,128]{1,0:T(8,128)(2,1)} copy(bf16[128,128]{1,0:T(8,128)(2,1)S(1)} %get-tuple-element.10) | data formatting | bytes 65536
  20.9 0.6 %copy.16 = bf16[128,128]{1,0:T(8,128)(2,1)} copy(bf16[128,128]{1,0:T(8,128)(2,1)S(1)} %get-tuple-element.11) | data formatting | bytes 65536
Async XLA Ops:
  0.6 0.9 %copy-start = (bf16[128,512]{1,0:T(8,128)(2,1)S(1)}, bf16[128,512]{1,0:T(8,128)(2,1)}, u32[]{:S(2)}) copy-start(bf16[128,512]{1,0:T(8,128)(2,1)} %q_hbm.1) | copy-start | bytes 393220
  1.5 0.9 %copy-start.1 = (bf16[128,512]{1,0:T(8,128)(2,1)S(1)}, bf16[128,512]{1,0:T(8,128)(2,1)}, u32[]{:S(2)}) copy-start(bf16[128,512]{1,0:T(8,128)(2,1)} %g_hbm.1) | copy-start | bytes 393220
  2.4 0.8 %copy-start.2 = (bf16[128,128]{1,0:T(8,128)(2,1)S(1)}, bf16[128,128]{1,0:T(8,128)(2,1)}, u32[]{:S(2)}) copy-start(bf16[128,128]{1,0:T(8,128)(2,1)} %k_hbm.1) | copy-start | bytes 98308
  3.2 0.8 %copy-start.3 = (bf16[128,128]{1,0:T(8,128)(2,1)S(1)}, bf16[128,128]{1,0:T(8,128)(2,1)}, u32[]{:S(2)}) copy-start(bf16[128,128]{1,0:T(8,128)(2,1)} %v_hbm.1) | copy-start | bytes 98308
  4.0 0.7 %copy-start.4 = (s32[32]{0:T(128)S(1)}, s32[32]{0:T(128)}, u32[]{:S(2)}) copy-start(s32[32]{0:T(128)} %lens_ref.1) | copy-start | bytes 388

commit v2 on v1

--- a/solution.py
+++ b/solution.py
@@ -214,7 +214,7 @@
 def near_kernel(
     n_ctx,
     n_head,
-    lens_ref,
+    lens_hbm,
     q_hbm,
     k_hbm,
     v_hbm,
@@ -223,6 +223,7 @@
     dq_ref,
     dk_ref,
     dv_ref,
+    lens_ref,
     q_ref,
     g_ref,
     kv_ref,
@@ -274,12 +275,41 @@
     loads = [
         pltpu.make_async_copy(k_hbm, kv_ref.at[:, pl.ds(0, width)], load_sem.at[0]),
         pltpu.make_async_copy(v_hbm, kv_ref.at[:, pl.ds(width, width)], load_sem.at[1]),
-        pltpu.make_async_copy(q_hbm, q_ref, load_sem.at[2]),
-        pltpu.make_async_copy(g_hbm, g_ref, load_sem.at[3]),
+        pltpu.make_async_copy(lens_hbm, lens_ref, load_sem.at[2]),
+        pltpu.make_async_copy(q_hbm, q_ref, load_sem.at[3]),
+        pltpu.make_async_copy(g_hbm, g_ref, load_sem.at[4]),
     ]
     for load in loads:
         load.start()
 
+    loads[0].wait()
+    loads[1].wait()
+    pl.semaphore_wait(
+        barrier,
+        (n_head - 1) + n_head * has_prev.astype(jnp.int32) + n_head * has_next.astype(jnp.int32),
+    )
+
+    def kv_copy(part, step):
+        return pltpu.make_async_remote_copy(
+            src_ref=kv_ref.at[pl.ds(part * st, st), :],
+            dst_ref=halo_ref.at[part],
+            send_sem=kv_send_sem.at[part],
+            recv_sem=kv_recv_sem.at[part],
+            device_id=(c + step, h),
+            device_id_type=MESH,
+        )
+
+    lower_kv, upper_kv = kv_copy(0, 1), kv_copy(1, -1)
+
+    @pl.when(has_next)
+    def _():
+        lower_kv.start()
+
+    @pl.when(has_prev)
+    def _():
+        upper_kv.start()
+
+    loads[2].wait()
     lane = lax.broadcasted_iota(jnp.int32, (1, rows), 1)
     place = lax.rem(lane, st)
     key_row = lax.broadcasted_iota(jnp.int32, (2 * st, rows), 0)
@@ -295,35 +325,8 @@
         for base, start in zip(bases, starts)
     ]
 
-    loads[0].wait()
-    loads[1].wait()
-    pl.semaphore_wait(
-        barrier,
-        (n_head - 1) + n_head * has_prev.astype(jnp.int32) + n_head * has_next.astype(jnp.int32),
-    )
-
-    def kv_copy(part, step):
-        return pltpu.make_async_remote_copy(
-            src_ref=kv_ref.at[pl.ds(part * st, st), :],
-            dst_ref=halo_ref.at[part],
-            send_sem=kv_send_sem.at[part],
-            recv_sem=kv_recv_sem.at[part],
-            device_id=(c + step, h),
-            device_id_type=MESH,
-        )
-
-    lower_kv, upper_kv = kv_copy(0, 1), kv_copy(1, -1)
-
-    @pl.when(has_next)
-    def _():
-        lower_kv.start()
-
-    @pl.when(has_prev)
-    def _():
-        upper_kv.start()
-
-    loads[2].wait()
     loads[3].wait()
+    loads[4].wait()
 
     def stacked(ref, part):
         return jnp.concatenate(
@@ -501,6 +504,18 @@
         copy.wait_send()
 
 
+def write_kernel(*refs):
+    sources, targets, sems = refs[:4], refs[4:8], refs[8]
+    copies = [
+        pltpu.make_async_copy(source, target, sems.at[i])
+        for i, (source, target) in enumerate(zip(sources, targets))
+    ]
+    for copy in copies:
+        copy.start()
+    for copy in copies:
+        copy.wait()
+
+
 def near_body(n_ctx, n_head, query, key, value, grad_out, doc_lengths):
     tok, width = key.shape
     st = tok // 2
@@ -508,18 +523,19 @@
     bf16, f32 = jnp.bfloat16, jnp.float32
     dma = pltpu.SemaphoreType.DMA
     vmem = pl.BlockSpec(memory_space=pltpu.VMEM)
-    hbm = pl.BlockSpec(memory_space=pl.ANY)
-    return pl.pallas_call(
+    hbm = pl.BlockSpec(memory_space=pltpu.HBM)
+    results = pl.pallas_call(
         functools.partial(near_kernel, n_ctx, n_head),
         out_shape=(
-            jax.ShapeDtypeStruct(query.shape, bf16),
-            jax.ShapeDtypeStruct(query.shape, bf16),
-            jax.ShapeDtypeStruct(key.shape, bf16),
-            jax.ShapeDtypeStruct(key.shape, bf16),
+            pltpu.VMEM(query.shape, bf16),
+            pltpu.VMEM(query.shape, bf16),
+            pltpu.VMEM(key.shape, bf16),
+            pltpu.VMEM(key.shape, bf16),
         ),
-        in_specs=[pl.BlockSpec(memory_space=pltpu.SMEM), hbm, hbm, hbm, hbm],
-        out_specs=(vmem, vmem, vmem, vmem),
+        in_specs=[hbm] * 5,
+        out_specs=(vmem,) * 4,
         scratch_shapes=[
+            pltpu.SMEM(doc_lengths.shape, jnp.int32),
             pltpu.VMEM(query.shape, bf16),
             pltpu.VMEM(query.shape, bf16),
             pltpu.VMEM((tok, 2 * width), bf16),
@@ -530,7 +546,7 @@
             pltpu.VMEM((n_head - 1, quarter, 2 * width), bf16),
             pltpu.VMEM((n_head, quarter, 2 * width), bf16),
             pltpu.VMEM((tok, 2 * width), bf16),
-            dma((4,)),
+            dma((5,)),
             dma((2,)),
             dma((2,)),
             dma((n_head - 1,)),
@@ -541,9 +557,18 @@
             dma((n_head - 1,)),
         ],
         compiler_params=pltpu.CompilerParams(
-            collective_id=0, has_side_effects=True, vmem_limit_bytes=16 * 1024 * 1024
+            collective_id=0, has_side_effects=True, vmem_limit_bytes=60 * 1024 * 1024
         ),
     )(doc_lengths, query, key, value, grad_out)
+    return pl.pallas_call(
+        write_kernel,
+        out_shape=tuple(jax.ShapeDtypeStruct(a.shape, bf16) for a in (query, query, key, key)),
+        in_specs=[vmem] * 4,
+        out_specs=(hbm,) * 4,
+        scratch_shapes=[dma((4,))],
+        compiler_params=pltpu.CompilerParams(vmem_limit_bytes=1024 * 1024),
+        name="write_out",
+    )(*results)
 
 
 def solution(mesh):

time: 21.8 us -> 15.4 us (0.71)
  local copies, waits for them, and re-layouts: 6.51 us -> 0 us
    unnamed x14 -> x0, local copies, waits for them, and re-layouts: 6.51 us -> none
    pallas_call x0 -> x1, Pallas kernels: none -> 0.75 us  [near_body(): pl.pallas_call(write_kernel, out_shape=tuple((jax.ShapeDtypeStruct(a.shap...]
    pallas_call x1, Pallas kernels: 14.4 us -> 13.9 us  [near_body(): pl.pallas_call(functools.partial(near_kernel, n_ctx, n_head), out_shape=(...]
where the time goes in v2:
time: 15.4 us; the launch traced here: 15.3 us
  Pallas kernels  14.6 us (95%)
  between operations  0.64 us (4%)
    pallas_call x1, Pallas kernels, near_body(): pl.pallas_call(functools.partial(near_kernel, n_ctx, n_head), out_shape=(...  13.9 us
    pallas_call x1, Pallas kernels, near_body(): pl.pallas_call(write_kernel, out_shape=tuple((jax.ShapeDtypeStruct(a.shap...  0.75 us

profile of v2, /device:TPU:0, one launch (start us, length us, event | category | flops | bytes accessed | tf_op | source)
XLA Modules:
  0.0 15.3 jit_solution(11394171662456352623)
XLA Ops:
  0.6 13.9 %shard_map.84 = (bf16[128,512]{1,0:T(8,128)(2,1)S(1)}, bf16[128,512]{1,0:T(8,128)(2,1)S(1)}, bf16[128,128]{1,0:T(8,128)(2,1)S(1)}, bf16[128,128]{1,0:T(8,128)(2,1)S(1)}) custom-call(s32[32]{0:T(128)} %lens_hbm.1, bf16[128,512]{1,0:T(8,128)(2,1)} %q_hbm.1, bf16[128,128]{1,0:T(8,128)(2,1)} %k_hbm.1, bf16[128,128]{1,0:T(8,128)(2,1)} %v_hbm.1, ...), custom_call_target="tpu_custom_call" | custom-call | tf_op jit(solution)/shard_map/pallas_call | solution.py:527
  14.5 0.7 %write_out.1 = (bf16[128,512]{1,0:T(8,128)(2,1)}, bf16[128,512]{1,0:T(8,128)(2,1)}, bf16[128,128]{1,0:T(8,128)(2,1)}, bf16[128,128]{1,0:T(8,128)(2,1)}) custom-call(bf16[128,512]{1,0:T(8,128)(2,1)S(1)} %get-tuple-element.8.refs_0_, bf16[128,512]{1,0:T(8,128)(2,1)S(1)} %get-tuple-element.9.refs_1_, bf16[128,128]{1,0:T(8,128)(2,1)S(1)} %get-tuple-element.10.refs_2_, ...), custom_call_target="tpu_custom_call" | custom-call | tf_op jit(solution)/shard_map/write_out/pallas_call | solution.py:563

commit v3 on v2

--- a/solution.py
+++ b/solution.py
@@ -257,20 +257,20 @@
     has_next = c < n_ctx - 1
 
     barrier = pltpu.get_barrier_semaphore()
+    @pl.when(has_prev)
+    def _():
+        for d in range(n_head):
+            pl.semaphore_signal(barrier, inc=1, device_id=(c - 1, d), device_id_type=MESH)
+
+    @pl.when(has_next)
+    def _():
+        for d in range(n_head):
+            pl.semaphore_signal(barrier, inc=1, device_id=(c + 1, d), device_id_type=MESH)
+
     for d in range(1, n_head):
         pl.semaphore_signal(
             barrier, inc=1, device_id=(c, lax.rem(h + d, n_head)), device_id_type=MESH
         )
-
-    @pl.when(has_prev)
-    def _():
-        for d in range(n_head):
-            pl.semaphore_signal(barrier, inc=1, device_id=(c - 1, d), device_id_type=MESH)
-
-    @pl.when(has_next)
-    def _():
-        for d in range(n_head):
-            pl.semaphore_signal(barrier, inc=1, device_id=(c + 1, d), device_id_type=MESH)
 
     loads = [
         pltpu.make_async_copy(k_hbm, kv_ref.at[:, pl.ds(0, width)], load_sem.at[0]),
@@ -357,6 +357,18 @@
         jnp.where(has_prev, halo_ref[0], zero),
         jnp.where(has_next, halo_ref[1], kv_ref[0:st, :]),
     ]
+    def halo_copy(part, j, step):
+        return pltpu.make_async_remote_copy(
+            src_ref=halo_send.at[part, pl.ds(j * quarter, quarter), :],
+            dst_ref=halo_recv.at[h],
+            send_sem=hs_send_sem.at[part, j],
+            recv_sem=hs_recv_sem.at[h],
+            device_id=(c + step, part * per_half + j),
+            device_id_type=MESH,
+        )
+
+    down = [halo_copy(0, j, -1) for j in range(per_half)]
+    up = [halo_copy(1, j, 1) for j in range(per_half)]
     scale = width ** (-0.5)
     probs, dscores, keys, values, grads = [], [], [], [], []
     for part in range(2):
@@ -377,38 +389,19 @@
         keys.append(jnp.concatenate([k_halo, k_own[part]], axis=0))
         values.append(jnp.concatenate([v_halo, v_own[part]], axis=0))
         grads.append(jnp.concatenate([grad_k, grad_v], axis=1))
+        halo_send[part] = grads[part][:st].astype(jnp.bfloat16)
+
+        @pl.when((has_prev, has_next)[part])
+        def _(part=part):
+            for copy in (down, up)[part]:
+                copy.start()
+
 
     lower = grads[0][st:] + jnp.where(has_next, 0.0, grads[1][:st])
     own_part[0:st, :] = lower
     own_part[st:tok, :] = grads[1][st:]
     own_send[0:st, :] = lower.astype(jnp.bfloat16)
     own_send[st:tok, :] = grads[1][st:].astype(jnp.bfloat16)
-    halo_send[0] = grads[0][:st].astype(jnp.bfloat16)
-    halo_send[1] = grads[1][:st].astype(jnp.bfloat16)
-
-    def halo_copy(part, j, step):
-        return pltpu.make_async_remote_copy(
-            src_ref=halo_send.at[part, pl.ds(j * quarter, quarter), :],
-            dst_ref=halo_recv.at[h],
-            send_sem=hs_send_sem.at[part, j],
-            recv_sem=hs_recv_sem.at[h],
-            device_id=(c + step, part * per_half + j),
-            device_id_type=MESH,
-        )
-
-    down = [halo_copy(0, j, -1) for j in range(per_half)]
-    up = [halo_copy(1, j, 1) for j in range(per_half)]
-
-    @pl.when(has_prev)
-    def _():
-        for copy in down:
-            copy.start()
-
-    @pl.when(has_next)
-    def _():
-        for copy in up:
-            copy.start()
-
     own_copies = []
     for d in range(1, n_head):
         peer = lax.rem(h + d, n_head)

time: 15.4 us -> 15.3 us (level)
  no operation moved by 1% of the time
where the time goes in v3:
time: 15.3 us; the launch traced here: 15.2 us
  Pallas kernels  14.6 us (95%)
  between operations  0.64 us (4%)
    pallas_call x1, Pallas kernels, near_body(): pl.pallas_call(functools.partial(near_kernel, n_ctx, n_head), out_shape=(...  13.8 us
    pallas_call x1, Pallas kernels, near_body(): pl.pallas_call(write_kernel, out_shape=tuple((jax.ShapeDtypeStruct(a.shap...  0.75 us

profile of v3, /device:TPU:0, one launch (start us, length us, event | category | flops | bytes accessed | tf_op | source)
XLA Modules:
  0.0 15.2 jit_solution(5148404085409909763)
XLA Ops:
  0.6 13.8 %shard_map.84 = (bf16[128,512]{1,0:T(8,128)(2,1)S(1)}, bf16[128,512]{1,0:T(8,128)(2,1)S(1)}, bf16[128,128]{1,0:T(8,128)(2,1)S(1)}, bf16[128,128]{1,0:T(8,128)(2,1)S(1)}) custom-call(s32[32]{0:T(128)} %lens_hbm.1, bf16[128,512]{1,0:T(8,128)(2,1)} %q_hbm.1, bf16[128,128]{1,0:T(8,128)(2,1)} %k_hbm.1, bf16[128,128]{1,0:T(8,128)(2,1)} %v_hbm.1, ...), custom_call_target="tpu_custom_call" | custom-call | tf_op jit(solution)/shard_map/pallas_call | solution.py:520
  14.4 0.7 %write_out.1 = (bf16[128,512]{1,0:T(8,128)(2,1)}, bf16[128,512]{1,0:T(8,128)(2,1)}, bf16[128,128]{1,0:T(8,128)(2,1)}, bf16[128,128]{1,0:T(8,128)(2,1)}) custom-call(bf16[128,512]{1,0:T(8,128)(2,1)S(1)} %get-tuple-element.8.refs_0_, bf16[128,512]{1,0:T(8,128)(2,1)S(1)} %get-tuple-element.9.refs_1_, bf16[128,128]{1,0:T(8,128)(2,1)S(1)} %get-tuple-element.10.refs_2_, ...), custom_call_target="tpu_custom_call" | custom-call | tf_op jit(solution)/shard_map/write_out/pallas_call | solution.py:556
